TPU v7x, 512 devices: a whole 4x8x8 slice. The times are simulated.
512 devices in a mesh: lon: 32 (over z_lo, y, core), ch: 16 (over x, z_hi).
Axes of the slice: x: 4, y: 8, z: 8 (z_hi: 4, z_lo: 2; z = z_hi * 2 + z_lo), core: 2. Of those that a mesh axis runs over, the one named last changes fastest.
Arguments:
- grid_state: bfloat16 [128, 512, 1024], P(None, 'lon', 'ch'), may hold values from -40 to 40
- first_gain: bfloat16 [1024], P('ch'), may hold values from 0.099609375 to 1.8984375
- spectral_first: bfloat16 [2, 1024, 64], P(None, 'ch'), may hold values from -0.5 to 0.5
- spectral_second: bfloat16 [2, 1024, 64], P(None, 'ch'), may hold values from -0.5 to 0.5
- second_gain: bfloat16 [1024], P('ch'), may hold values from 0.099609375 to 1.8984375
- up_weight: bfloat16 [1024, 4096], P(None, 'ch'), may hold values from -0.1875 to 0.1875
- down_weight: bfloat16 [4096, 1024], P('ch'), may hold values from -0.125 to 0.125
Outputs:
- block_out: bfloat16 [128, 512, 1024], P(None, 'lon', 'ch')
All inputs are finite; a program needn't handle non-finite values.
Results may differ from a plain program's by a relative error of at most 0.015.
Values may be sent and summed in bfloat16 or wider, within the bound.
No kernel may reach another device: no remote copies, remote signals or barrier semaphores. Data moves between devices by JAX's collectives and lax.ppermute only.
A program may use at most 64 MiB of HBM per device.

v0:
```python
import math
import jax
import jax.numpy as jnp
from jax import lax
from jax.sharding import PartitionSpec as P

H = 128
W = 512
C = 1024
KW = 256
EPSILON = 1e-05
THRESHOLD = 0.1
HIGHEST = lax.Precision.HIGHEST


def dft_tables(length, harmonics):
    sample_idx = jnp.arange(length, dtype=jnp.int32)[:, None]
    harmonic_idx = jnp.arange(harmonics, dtype=jnp.int32)[None, :]
    phase = (sample_idx * harmonic_idx % length).astype(jnp.float32) * (2.0 * math.pi / length)
    factor = 1.0 / math.sqrt(length)
    return (jnp.cos(phase) * factor, jnp.sin(phase) * factor)


def normalize(values, total, square, gain, width):
    centre = total[..., None] / width
    spread = square[..., None] / width - centre * centre
    return ((values - centre) * lax.rsqrt(spread + EPSILON) * gain).astype(jnp.bfloat16)


def soft_shrink(values):
    return values - jnp.clip(values, -THRESHOLD, THRESHOLD)


def lat_apply(values, table):
    return jnp.einsum("kch,hq->kcq", values, table, precision=HIGHEST)


def complex_mix(real_part, imag_part, weight):
    mode_len, chan_len, lat_len = real_part.shape
    block_width = weight.shape[-1]
    blocks = chan_len // block_width
    w_real = weight[0].reshape(blocks, block_width, block_width)
    w_imag = weight[1].reshape(blocks, block_width, block_width)
    real_blocks = real_part.reshape(mode_len, blocks, block_width, lat_len)
    imag_blocks = imag_part.reshape(mode_len, blocks, block_width, lat_len)

    def product(left, right):
        return jnp.einsum("knbq,nbd->kndq", left, right, preferred_element_type=jnp.float32)

    new_real = product(real_blocks, w_real) - product(imag_blocks, w_imag)
    new_imag = product(real_blocks, w_imag) + product(imag_blocks, w_real)
    return (
        new_real.reshape(mode_len, chan_len, lat_len),
        new_imag.reshape(mode_len, chan_len, lat_len),
    )


def per_device(
    grid_state, first_gain, spectral_first, spectral_second, second_gain, up_weight, down_weight
):
    lat_count, col_count, chan_count = grid_state.shape
    values = grid_state.astype(jnp.float32)
    total_one, square_one = lax.psum(
        (jnp.sum(values, axis=2), jnp.sum(values * values, axis=2)), "ch"
    )
    normed_first = normalize(values, total_one, square_one, first_gain, C)
    columns = lax.all_to_all(normed_first, "lon", split_axis=2, concat_axis=1, tiled=True)
    lon_cos, lon_sin = dft_tables(W, KW)
    lat_cos, lat_sin = dft_tables(H, H)
    column_data = columns.astype(jnp.float32)
    fwd_real = jnp.einsum("hwc,wk->kch", column_data, lon_cos, precision=HIGHEST)
    fwd_imag = -jnp.einsum("hwc,wk->kch", column_data, lon_sin, precision=HIGHEST)
    spec_real = lat_apply(fwd_real, lat_cos) + lat_apply(fwd_imag, lat_sin)
    spec_imag = lat_apply(fwd_imag, lat_cos) - lat_apply(fwd_real, lat_sin)
    modes = lax.all_to_all(
        jnp.stack([spec_real, spec_imag]).astype(jnp.bfloat16),
        "lon",
        split_axis=1,
        concat_axis=2,
        tiled=True,
    )
    mid_real, mid_imag = complex_mix(modes[0], modes[1], spectral_first)
    mid_real = jax.nn.relu(mid_real).astype(jnp.bfloat16)
    mid_imag = jax.nn.relu(mid_imag).astype(jnp.bfloat16)
    out_real, out_imag = complex_mix(mid_real, mid_imag, spectral_second)
    out_real = soft_shrink(out_real)
    out_imag = soft_shrink(out_imag)
    inv_real = lat_apply(out_real, lat_cos) - lat_apply(out_imag, lat_sin)
    inv_imag = lat_apply(out_imag, lat_cos) + lat_apply(out_real, lat_sin)
    returned = lax.all_to_all(
        jnp.stack([inv_real, inv_imag]).astype(jnp.bfloat16),
        "lon",
        split_axis=2,
        concat_axis=1,
        tiled=True,
    ).astype(jnp.float32)
    back_real = returned[0]
    back_imag = returned[1]
    harmonic_weight = jnp.where(jnp.arange(KW, dtype=jnp.int32) == 0, 1.0, 2.0).astype(jnp.float32)
    inv_cos = lon_cos * harmonic_weight[None, :]
    inv_sin = lon_sin * harmonic_weight[None, :]
    grid_cols = jnp.einsum("kch,wk->hwc", back_real, inv_cos, precision=HIGHEST)
    grid_cols = grid_cols - jnp.einsum("kch,wk->hwc", back_imag, inv_sin, precision=HIGHEST)
    filtered = lax.all_to_all(
        grid_cols.astype(jnp.bfloat16), "lon", split_axis=1, concat_axis=2, tiled=True
    )
    mixed = (values + normed_first.astype(jnp.float32) + filtered.astype(jnp.float32)).astype(
        jnp.bfloat16
    )
    mixed_wide = mixed.astype(jnp.float32)
    token_count = lat_count * col_count
    everything, whole_gain = (
        lax.all_gather(mixed, "ch", axis=2, tiled=True),
        lax.all_gather(second_gain, "ch", axis=0, tiled=True),
    )
    spread_all = everything.astype(jnp.float32)
    normed_second = normalize(
        spread_all,
        jnp.sum(spread_all, axis=2),
        jnp.sum(spread_all * spread_all, axis=2),
        whole_gain,
        C,
    )
    upward = jnp.dot(
        normed_second.reshape(token_count, C), up_weight, preferred_element_type=jnp.float32
    )
    hidden = jax.nn.gelu(upward).astype(jnp.bfloat16)
    summed = lax.psum_scatter(
        jnp.einsum("tj,jc->ct", hidden, down_weight, preferred_element_type=jnp.float32).astype(
            jnp.bfloat16
        ),
        "ch",
        scatter_dimension=0,
        tiled=True,
    ).astype(jnp.float32)
    branch = summed.T.reshape(lat_count, col_count, chan_count)
    return (mixed_wide + branch).astype(jnp.bfloat16)


def solution(mesh):
    return jax.shard_map(
        per_device,
        mesh=mesh,
        in_specs=(
            P(None, "lon", "ch"),
            P("ch"),
            P(None, "ch", None),
            P(None, "ch", None),
            P("ch"),
            P(None, "ch"),
            P("ch", None),
        ),
        out_specs=P(None, "lon", "ch"),
        check_vma=False,
    )
```

profile of v0, /device:TPU:1, one launch (start us, length us, event | category | flops | bytes accessed | tf_op | source)
XLA Modules:
  0.0 401.5 jit_solution(9092841457983095221)
XLA Ops:
  6.5 1.2 convert_reduce_fusion.1
  7.7 0.7 convert_element_type.105
  8.4 74.7 %all-reduce.1 = (f32[128,16]{0,1:T(8,128)S(1)}, f32[128,16]{0,1:T(8,128)S(1)}) all-reduce(f32[128,16]{0,1:T(8,128)S(1)} %get-tuple-element.8, f32[128,16]{0,1:T(8,128)S(1)} %get-tuple-element.7), channel_id=1, replica_groups=mesh['lon'=32,'ch'=16] {'ch'}, use_global_device_ids=true, to_apply=%region_3.0 | all-reduce | flops 4096 | bytes 32768 | tf_op jit(solution)/shard_map/psum | solution.py:63
  83.0 1.1 fusion.41
  84.2 34.5 %all_to_all.57 = bf16[128,16,64]{0,1,2:T(8,128)(2,1)S(1)} all-to-all(bf16[128,16,64]{0,1,2:T(8,128)(2,1)S(1)} %fusion.41), channel_id=1, replica_groups=mesh['lon'=32,'ch'=16] {'lon'}, dimensions={2} | all-to-all | bytes 524288 | tf_op jit(solution)/shard_map/all_to_all | solution.py:67
  118.8 2.7 convolution_bitcast_fusion
  121.4 2.7 fusion.17
  124.1 0.6 fusion.80
  124.8 0.6 fusion.78
  125.4 0.6 fusion.30
  126.0 0.6 fusion.29
  127.0 16.2 %all_to_all.58 = bf16[2,256,2,128]{3,2,0,1:T(2,128)(2,1)S(1)} all-to-all(bf16[2,256,2,128]{3,2,0,1:T(2,128)(2,1)S(1)} %copy.123), channel_id=1, replica_groups=mesh['lon'=32,'ch'=16] {'lon'}, dimensions={1} | all-to-all | bytes 524288 | tf_op jit(solution)/shard_map/all_to_all | solution.py:75
  146.5 0.6 fusion.28
  147.2 0.6 fusion.27
  147.8 0.9 copy.129
  148.7 5.0 %all-to-all-start.2 = ((bf16[2,8,64,128]{3,1,0,2:T(8,128)(2,1)}), bf16[2,8,64,128]{3,1,0,2:T(8,128)(2,1)S(1)}, u32[]{:S(2)}, u32[]{:S(2)}) async-start(bf16[2,8,64,128]{3,1,0,2:T(8,128)(2,1)} %copy.129), calls=%async_computation.2 | async-start | bytes 524288 | tf_op jit(solution)/shard_map/all_to_all | solution.py:90
  154.0 11.8 %all-to-all-done.2 = bf16[2,8,64,128]{3,1,0,2:T(8,128)(2,1)S(1)} async-done(((bf16[2,8,64,128]{3,1,0,2:T(8,128)(2,1)}), bf16[2,8,64,128]{3,1,0,2:T(8,128)(2,1)S(1)}, u32[]{:S(2)}, u32[]{:S(2)}) %all-to-all-start.2) | async-done | bytes 262176 | tf_op jit(solution)/shard_map/all_to_all | solution.py:90
  165.8 2.3 fusion.48
  168.1 2.5 fusion.18
  170.9 16.2 %all_to_all.59 = bf16[128,512,2]{0,2,1:T(2,128)(2,1)S(1)} all-to-all(bf16[128,512,2]{0,2,1:T(2,128)(2,1)S(1)} %copy.131), channel_id=1, replica_groups=mesh['lon'=32,'ch'=16] {'lon'}, dimensions={1} | all-to-all | bytes 524288 | tf_op jit(solution)/shard_map/all_to_all | solution.py:104
  187.3 0.9 fusion.44
  188.3 1.3 dynamic-slice
  190.4 32.4 %all-reduce = bf16[1024]{0:T(1024)(128)(2,1)S(1)} all-reduce(bf16[1024]{0:T(1024)(128)(2,1)S(1)} %dynamic-update-slice), channel_id=1, replica_groups=mesh['lon'=32,'ch'=16] {'ch'}, use_global_device_ids=true, to_apply=%add | all-reduce | flops 1024 | bytes 4096
  222.8 37.9 %all-gather.2.cloned.1.call-done = bf16[128,16,1024]{0,1,2:T(8,128)(2,1)} async-done(((bf16[128,16,64]{0,1,2:T(8,128)(2,1)}), bf16[128,16,1024]{0,1,2:T(8,128)(2,1)}) %all-gather.2.cloned.1.call-update) | async-done | bytes 4194320 | tf_op jit(solution)/shard_map/all_gather | solution.py:113
  260.7 7.4 %copy.134 = bf16[128,16,1024]{2,1,0:T(8,128)(2,1)} copy(bf16[128,16,1024]{0,1,2:T(8,128)(2,1)} %all-gather.2.cloned.1.call-done) | data formatting | bytes 8388608 | tf_op jit(solution)/shard_map/all_gather | solution.py:113
  268.2 3.6 convert_reduce_fusion
  272.1 4.4 %fusion.2 = bf16[128,16,1024]{2,1,0:T(8,128)(2,1)} fusion(bf16[128,16,1024]{2,1,0:T(8,128)(2,1)} %copy.134, f32[1024]{0:T(1024)S(1)} %convert_element_type.123, f32[128,16]{1,0:T(8,128)S(1)} %copy.138, f32[128,16]{1,0:T(8,128)S(1)} %copy.136), kind=kLoop, calls=%fused_computation.5 | loop fusion | flops 10485760 | bytes 8409088 | tf_op jit(solution)/shard_map/convert_element_type | solution.py:27
  276.5 8.5 %convert_bitcast_fusion = bf16[1024,2048]{0,1:T(8,128)(2,1)} fusion(bf16[256,1024]{1,0:T(8,128)(2,1)S(1)} %copy-done, bf16[2048,1024]{1,0:T(8,128)(2,1)} %bitcast.168, bf16[1024,256]{1,0:T(8,128)(2,1)S(1)} %copy-done.5), kind=kOutput, calls=%fused_computation.7 | convolution fusion | flops 2154299392 | bytes 9437184 | tf_op jit(solution)/shard_map/tj,jc->ct/dot_general | solution.py:129
  284.9 6.5 %copy.147 = bf16[1024,2048]{1,0:T(8,128)(2,1)} copy(bf16[1024,2048]{0,1:T(8,128)(2,1)} %convert_bitcast_fusion) | data formatting | bytes 8388608
  291.5 100.5 %reduce-scatter.4.cloned.1.call-done = bf16[64,2048]{1,0:T(8,128)(2,1)} async-done(((bf16[1024,2048]{1,0:T(8,128)(2,1)}), bf16[64,2048]{1,0:T(8,128)(2,1)}) %reduce-scatter.4.cloned.1.call-update) | async-done | bytes 262160
  392.0 1.2 copy.148
  393.9 0.8 copy.140
  (52 shorter events, 5.7 us)
Async XLA Ops:
  6.5 269.9 %copy-start = (bf16[256,1024]{1,0:T(8,128)(2,1)S(1)}, bf16[256,1024]{1,0:T(8,128)(2,1)}, u32[]{:S(2)}) copy-start(bf16[256,1024]{1,0:T(8,128)(2,1)} %param.13) | copy-start | bytes 1572868
  121.4 22.1 %copy-start.3 = (bf16[2,64,64]{2,1,0:T(8,128)(2,1)S(1)}, bf16[2,64,64]{2,1,0:T(8,128)(2,1)}, u32[]{:S(2)}) copy-start(bf16[2,64,64]{2,1,0:T(8,128)(2,1)} %param.9) | copy-start | bytes 49156
  121.4 22.8 %copy-start.4 = (bf16[2,64,64]{2,1,0:T(8,128)(2,1)S(1)}, bf16[2,64,64]{2,1,0:T(8,128)(2,1)}, u32[]{:S(2)}) copy-start(bf16[2,64,64]{2,1,0:T(8,128)(2,1)} %param.10) | copy-start | bytes 49156
  148.7 17.1 %all-to-all-start.2 = ((bf16[2,8,64,128]{3,1,0,2:T(8,128)(2,1)}), bf16[2,8,64,128]{3,1,0,2:T(8,128)(2,1)S(1)}, u32[]{:S(2)}, u32[]{:S(2)}) async-start(bf16[2,8,64,128]{3,1,0,2:T(8,128)(2,1)} %copy.129), calls=%async_computation.2 | async-start | bytes 524288 | tf_op jit(solution)/shard_map/all_to_all | solution.py:90
  153.7 107.0 %all-gather.2.cloned.1.call-start = ((), (), s32[]{:S(2)}) async-start(), calls=%async_computation.5 | async-start | bytes 4456448 | tf_op jit(solution)/shard_map/all_gather | solution.py:113
  165.8 21.4 %copy-start.1 = (bf16[128,16,64]{0,2,1:T(8,128)(2,1)S(1)}, bf16[128,16,64]{0,2,1:T(8,128)(2,1)}, u32[]{:S(2)}) copy-start(bf16[128,16,64]{0,2,1:T(8,128)(2,1)} %param.7) | copy-start | bytes 786436
  168.1 22.1 %copy-start.6 = (bf16[64]{0:T(256)(128)(2,1)S(1)}, bf16[64]{0:T(256)(128)(2,1)}, u32[]{:S(2)}) copy-start(bf16[64]{0:T(256)(128)(2,1)} %param.11) | copy-start | bytes 388
  188.2 203.8 %reduce-scatter.4.cloned.1.call-start = ((), (), s32[]{:S(2)}) async-start(), calls=%async_computation.6 | async-start | bytes 4456448
  272.1 4.4 %copy-start.5 = (bf16[1024,256]{1,0:T(8,128)(2,1)S(1)}, bf16[1024,256]{1,0:T(8,128)(2,1)}, u32[]{:S(2)}) copy-start(bf16[1024,256]{1,0:T(8,128)(2,1)} %param.12) | copy-start | bytes 1572868
  291.5 102.4 %copy-start.2 = (bf16[128,16,64]{0,1,2:T(8,128)(2,1)S(1)}, bf16[128,16,64]{0,1,2:T(8,128)(2,1)}, u32[]{:S(2)}) copy-start(bf16[128,16,64]{0,1,2:T(8,128)(2,1)} %fusion.44) | copy-start | bytes 786436
Sparse Core Ops, SparseCore 0:
  188.3 72.3 all-gather.1
  291.6 100.3 reduce-scatter.3
where the time goes:
time: 402 us
  blocking collectives  174 us (43%)
  waiting for transfers between devices  150 us (37%)
  matrix products  25.2 us (6%)
  local copies, waits for them, and re-layouts  20.4 us (5%)
  between operations  14.4 us (4%)
  other arithmetic  12.1 us (3%)
  starting transfers between devices  5.27 us (1%)
    unnamed x3, waiting for transfers between devices  101 us
    psum x1, blocking collectives, per_device(): lax.psum((jnp.sum(values, axis=2), jnp.sum(values * values, axis=2)), 'ch')  74.7 us
    all_gather x1, waiting for transfers between devices, per_device(): lax.all_gather(mixed, 'ch', axis=2, tiled=True)  37.9 us
    all_to_all x1, blocking collectives, per_device(): lax.all_to_all(normed_first, 'lon', split_axis=2, concat_axis=1, tiled=True)  34.5 us
    unnamed x1, blocking collectives  32.4 us
    all_to_all x1, blocking collectives, per_device(): lax.all_to_all(grid_cols.astype(jnp.bfloat16), 'lon', split_axis=1, conca...  16.2 us
    all_to_all x1, blocking collectives, per_device(): lax.all_to_all(jnp.stack([spec_real, spec_imag]).astype(jnp.bfloat16), 'l...  16.2 us
    all_to_all x1, waiting for transfers between devices, per_device(): lax.all_to_all(jnp.stack([inv_real, inv_imag]).astype(jnp.bfloat16), 'lon...  11.8 us
  transfers between devices with their start and end apart: 3, of which 3 were waited for; matrix products, arithmetic and copies ran while one was open for 0% of the time, Pallas kernels for 0%

commit v1 on v0

--- a/solution.py
+++ b/solution.py
@@ -110,7 +110,9 @@
     mixed_wide = mixed.astype(jnp.float32)
     token_count = lat_count * col_count
     everything, whole_gain = (
-        lax.all_gather(mixed, "ch", axis=2, tiled=True),
+        jnp.concatenate(
+            lax.all_to_all(jnp.stack([mixed] * lax.axis_size("ch")), "ch", 0, 0), axis=2
+        ),
         lax.all_gather(second_gain, "ch", axis=0, tiled=True),
     )
     spread_all = everything.astype(jnp.float32)

time: 402 us -> 488 us (1.21)
  blocking collectives: 174 us -> 263 us
  waiting for transfers between devices: 150 us -> 115 us
  local copies, waits for them, and re-layouts: 20.4 us -> 46.8 us
    unnamed x1, blocking collectives: 32.4 us -> 122 us
    all_gather x1 -> x0, waiting for transfers between devices: 37.9 us -> none  [per_device(): lax.all_gather(mixed, 'ch', axis=2, tiled=True)]
    convert_element_type x0 -> x3, local copies, waits for them, and re-layouts: none -> 30.9 us  [the longest x2 30.8 us: per_device(): spread_all = everything.astype(jnp.float32)]
    all_gather x1 -> x0, local copies, waits for them, and re-layouts: 7.43 us -> none  [per_device(): lax.all_gather(mixed, 'ch', axis=2, tiled=True)]
    convert_element_type x1, other arithmetic: 0.04 us -> 6.48 us  [per_device(): spread_all = everything.astype(jnp.float32)]
    unnamed x3 -> x2, waiting for transfers between devices: 101 us -> 102 us
  transfers between devices with their start and end apart: 3 -> 3, of which waited for: 3 -> 2; matrix products, arithmetic and copies ran while one was open for 0% -> 0% of each run, Pallas kernels for 0% -> 0%
where the time goes in v1:
time: 488 us; the launch traced here: 487 us
  blocking collectives  263 us (54%)
  waiting for transfers between devices  115 us (24%)
  local copies, waits for them, and re-layouts  46.8 us (10%)
  matrix products  24.9 us (5%)
  between operations  14.4 us (3%)
  other arithmetic  13.2 us (3%)
  starting transfers between devices  9.72 us (2%)
    unnamed x1, blocking collectives  122 us
    unnamed x2, waiting for transfers between devices  102 us
    psum x1, blocking collectives, per_device(): lax.psum((jnp.sum(values, axis=2), jnp.sum(values * values, axis=2)), 'ch')  74.7 us
    all_to_all x1, blocking collectives, per_device(): lax.all_to_all(normed_first, 'lon', split_axis=2, concat_axis=1, tiled=True)  34.5 us
    convert_element_type x2, local copies, waits for them, and re-layouts, per_device(): spread_all = everything.astype(jnp.float32)  30.8 us
    all_to_all x1, blocking collectives, per_device(): lax.all_to_all(grid_cols.astype(jnp.bfloat16), 'lon', split_axis=1, conca...  16.2 us
    all_to_all x1, blocking collectives, per_device(): lax.all_to_all(jnp.stack([spec_real, spec_imag]).astype(jnp.bfloat16), 'l...  16.2 us
    all_to_all x1, waiting for transfers between devices, per_device(): lax.all_to_all(jnp.stack([inv_real, inv_imag]).astype(jnp.bfloat16), 'lon...  12 us
  transfers between devices with their start and end apart: 3, of which 2 were waited for; matrix products, arithmetic and copies ran while one was open for 0% of the time, Pallas kernels for 0%

profile of v1, /device:TPU:1, one launch (start us, length us, event | category | flops | bytes accessed | tf_op | source)
XLA Modules:
  0.0 486.8 jit_solution(6712168130532696609)
XLA Ops:
  6.5 1.2 convert_reduce_fusion
  7.7 0.7 convert_element_type.118
  8.4 74.7 %all-reduce.1 = (f32[128,16]{0,1:T(8,128)S(1)}, f32[128,16]{0,1:T(8,128)S(1)}) all-reduce(f32[128,16]{0,1:T(8,128)S(1)} %get-tuple-element.8, f32[128,16]{0,1:T(8,128)S(1)} %get-tuple-element.7), channel_id=1, replica_groups=mesh['lon'=32,'ch'=16] {'ch'}, use_global_device_ids=true, to_apply=%region_3.0 | all-reduce | flops 4096 | bytes 32768 | tf_op jit(solution)/shard_map/psum | solution.py:63
  83.0 1.1 fusion.41
  84.2 34.5 %all_to_all.62 = bf16[128,16,64]{0,1,2:T(8,128)(2,1)S(1)} all-to-all(bf16[128,16,64]{0,1,2:T(8,128)(2,1)S(1)} %fusion.41), channel_id=1, replica_groups=mesh['lon'=32,'ch'=16] {'lon'}, dimensions={2} | all-to-all | bytes 524288 | tf_op jit(solution)/shard_map/all_to_all | solution.py:67
  118.8 2.7 convolution_bitcast_fusion
  121.4 2.7 fusion.18
  124.1 0.6 fusion.80
  124.8 0.6 fusion.78
  125.4 0.6 fusion.31
  126.0 0.6 fusion.30
  127.0 16.2 %all_to_all.63 = bf16[2,256,2,128]{3,2,0,1:T(2,128)(2,1)S(1)} all-to-all(bf16[2,256,2,128]{3,2,0,1:T(2,128)(2,1)S(1)} %copy.86), channel_id=1, replica_groups=mesh['lon'=32,'ch'=16] {'lon'}, dimensions={1} | all-to-all | bytes 524288 | tf_op jit(solution)/shard_map/all_to_all | solution.py:75
  146.5 0.6 fusion.29
  147.8 0.9 copy.92
  148.7 5.0 %all-to-all-start.2 = ((bf16[2,8,64,128]{3,1,0,2:T(8,128)(2,1)}), bf16[2,8,64,128]{3,1,0,2:T(8,128)(2,1)S(1)}, u32[]{:S(2)}, u32[]{:S(2)}) async-start(bf16[2,8,64,128]{3,1,0,2:T(8,128)(2,1)} %copy.92), calls=%async_computation.2 | async-start | bytes 524288 | tf_op jit(solution)/shard_map/all_to_all | solution.py:90
  153.7 12.0 %all-to-all-done.2 = bf16[2,8,64,128]{3,1,0,2:T(8,128)(2,1)S(1)} async-done(((bf16[2,8,64,128]{3,1,0,2:T(8,128)(2,1)}), bf16[2,8,64,128]{3,1,0,2:T(8,128)(2,1)S(1)}, u32[]{:S(2)}, u32[]{:S(2)}) %all-to-all-start.2) | async-done | bytes 262176 | tf_op jit(solution)/shard_map/all_to_all | solution.py:90
  165.8 2.3 fusion.48
  168.1 2.5 fusion.19
  170.9 16.2 %all_to_all.64 = bf16[128,512,2]{0,2,1:T(2,128)(2,1)S(1)} all-to-all(bf16[128,512,2]{0,2,1:T(2,128)(2,1)S(1)} %copy.94), channel_id=1, replica_groups=mesh['lon'=32,'ch'=16] {'lon'}, dimensions={1} | all-to-all | bytes 524288 | tf_op jit(solution)/shard_map/all_to_all | solution.py:104
  187.5 3.0 stack.49
  190.5 4.7 all-to-all-start.4
  195.2 1.3 dynamic-slice
  197.4 121.7 %all-reduce = bf16[1024]{0:T(1024)(128)(2,1)S(1)} all-reduce(bf16[1024]{0:T(1024)(128)(2,1)S(1)} %dynamic-update-slice), channel_id=1, replica_groups=mesh['lon'=32,'ch'=16] {'ch'}, use_global_device_ids=true, to_apply=%add | all-reduce | flops 1024 | bytes 4096
  319.1 3.3 fusion.1
  322.8 6.5 %convert_bitcast_fusion = f32[128,16,16,64]{0,3,1,2:T(8,128)} fusion(bf16[16,128,16,64]{1,3,2,0:T(8,128)(2,1)} %all-to-all-done.4), kind=kLoop, calls=%fused_computation | loop fusion | flops 2097152 | bytes 12582912 | tf_op jit(solution)/shard_map/convert_element_type | solution.py:118
  329.3 16.3 %copy.97 = f32[128,16,16,64]{3,2,1,0:T(8,128)} copy(f32[128,16,16,64]{0,3,1,2:T(8,128)} %convert_bitcast_fusion) | data formatting | bytes 16777216 | tf_op jit(solution)/shard_map/convert_element_type | solution.py:118
  345.5 14.5 %reshape.147 = f32[2048,1024]{1,0:T(8,128)} reshape(f32[128,16,16,64]{3,2,1,0:T(8,128)} %copy.97) | data formatting | bytes 16777216 | tf_op jit(solution)/shard_map/convert_element_type | solution.py:118
  360.1 8.1 %convert_bitcast_fusion.1 = bf16[1024,2048]{0,1:T(8,128)(2,1)} fusion(bf16[256,1024]{1,0:T(8,128)(2,1)S(1)} %copy-done, bf16[1024,256]{1,0:T(8,128)(2,1)S(1)} %copy-done.4, f32[2048,1024]{1,0:T(8,128)} %reshape.147, f32[1024]{0:T(1024)S(1)} %convert_element_type.139, f32[2048]{0:T(1024)S(1)} %add_rsqrt_fusion, f32[2048]{0:T(1024)S(1)} %div.19), kind=kOutput, calls=%fused_computation.5 | convolution fusion | flops 2162688000 | bytes 13651968 | tf_op jit(solution)/shard_map/tj,jc->ct/dot_general | solution.py:131
  368.2 6.5 %copy.108 = bf16[1024,2048]{1,0:T(8,128)(2,1)} copy(bf16[1024,2048]{0,1:T(8,128)(2,1)} %convert_bitcast_fusion.1) | data formatting | bytes 8388608
  374.7 102.5 %reduce-scatter.4.cloned.1.call-done = bf16[64,2048]{1,0:T(8,128)(2,1)} async-done(((bf16[1024,2048]{1,0:T(8,128)(2,1)}), bf16[64,2048]{1,0:T(8,128)(2,1)}) %reduce-scatter.4.cloned.1.call-update) | async-done | bytes 262160
  477.2 1.2 copy.109
  479.2 0.8 copy.101
  (51 shorter events, 6.3 us)
Async XLA Ops:
  6.5 353.5 %copy-start = (bf16[256,1024]{1,0:T(8,128)(2,1)S(1)}, bf16[256,1024]{1,0:T(8,128)(2,1)}, u32[]{:S(2)}) copy-start(bf16[256,1024]{1,0:T(8,128)(2,1)} %param.13) | copy-start | bytes 1572868
  121.4 22.1 %copy-start.2 = (bf16[2,64,64]{2,1,0:T(8,128)(2,1)S(1)}, bf16[2,64,64]{2,1,0:T(8,128)(2,1)}, u32[]{:S(2)}) copy-start(bf16[2,64,64]{2,1,0:T(8,128)(2,1)} %param.9) | copy-start | bytes 49156
  121.4 22.8 %copy-start.3 = (bf16[2,64,64]{2,1,0:T(8,128)(2,1)S(1)}, bf16[2,64,64]{2,1,0:T(8,128)(2,1)}, u32[]{:S(2)}) copy-start(bf16[2,64,64]{2,1,0:T(8,128)(2,1)} %param.10) | copy-start | bytes 49156
  147.8 39.3 %copy-start.1 = (bf16[128,16,64]{0,2,1:T(8,128)(2,1)S(1)}, bf16[128,16,64]{0,2,1:T(8,128)(2,1)}, u32[]{:S(2)}) copy-start(bf16[128,16,64]{0,2,1:T(8,128)(2,1)} %param.7) | copy-start | bytes 786436
  148.7 17.1 %all-to-all-start.2 = ((bf16[2,8,64,128]{3,1,0,2:T(8,128)(2,1)}), bf16[2,8,64,128]{3,1,0,2:T(8,128)(2,1)S(1)}, u32[]{:S(2)}, u32[]{:S(2)}) async-start(bf16[2,8,64,128]{3,1,0,2:T(8,128)(2,1)} %copy.92), calls=%async_computation.2 | async-start | bytes 524288 | tf_op jit(solution)/shard_map/all_to_all | solution.py:90
  190.5 6.7 %copy-start.5 = (bf16[64]{0:T(256)(128)(2,1)S(1)}, bf16[64]{0:T(256)(128)(2,1)}, u32[]{:S(2)}) copy-start(bf16[64]{0:T(256)(128)(2,1)} %param.11) | copy-start | bytes 388
  190.5 128.6 %all-to-all-start.4 = ((bf16[16,128,16,64]{1,3,2,0:T(8,128)(2,1)}), bf16[16,128,16,64]{1,3,2,0:T(8,128)(2,1)}, u32[]{:S(2)}, u32[]{:S(2)}) async-start(bf16[16,128,16,64]{1,3,2,0:T(8,128)(2,1)} %stack.49), calls=%async_computation.4 | async-start | bytes 8388608 | tf_op jit(solution)/shard_map/all_to_all | solution.py:114
  195.2 282.1 %reduce-scatter.4.cloned.1.call-start = ((), (), s32[]{:S(2)}) async-start(), calls=%async_computation.6 | async-start | bytes 4456448
  345.5 14.6 %copy-start.4 = (bf16[1024,256]{1,0:T(8,128)(2,1)S(1)}, bf16[1024,256]{1,0:T(8,128)(2,1)}, u32[]{:S(2)}) copy-start(bf16[1024,256]{1,0:T(8,128)(2,1)} %param.12) | copy-start | bytes 1572868
Sparse Core Ops, SparseCore 0:
  374.9 102.3 reduce-scatter.3
